TPU v7x, 32 devices: a whole 2x2x4 slice. The times are simulated.
32 devices in a mesh: parts: 2 (over y), brick: 4 (over z), case: 4 (over x, core).
Axes of the slice: x: 2, y: 2, z: 4, core: 2. Of those that a mesh axis runs over, the one named last changes fastest.
Arguments:
- density: float32 [16, 64, 128], P(('parts', 'brick')), parts along dimension 0, may hold values from 0.3 to 1
- phase: int32 [16, 64, 128], P(('parts', 'brick')), parts along dimension 0, may hold values from 0 to 2
- warm_start: float32 [16, 3, 8, 64, 128], P(('parts', 'case'), None, 'brick'), parts along dimension 0, may hold values from -1.2 to 1.2
- case_table: int32 [8], replicated, may hold values from 0 to 7, each once
- multiplier: float32 [8, 8], replicated, may hold values from -1.5 to 1.5
- target: float32 [8, 8], replicated, may hold values from 0 to 0.4
- penalty_steps: int32 [8, 8], replicated, may hold values from 0 to 3
Outputs:
- fluctuation: float32 [16, 3, 8, 64, 128], P(('parts', 'case'), None, 'brick'), parts along dimension 0
- tensor: float32 [16, 8], P(('parts', 'case')), parts along dimension 0
- design_gradient: float32 [16, 64, 128], P(('parts', 'brick'), 'case'), parts along dimension 0
There are 2 independent parts, one for each index of `parts`. A program takes and returns all parts, laid end to end along the dimension named above; an argument that names none is the same for every part. Nothing has to cross between parts.
Inputs may be any that keep to these rules, and one draw needn't show every extreme that they name: `case_table`: a permutation of 0 to 7: values 0 to 5 name the six unit strains once each, larger values mark padded cases.
All inputs are finite; a program needn't handle non-finite values.
Results may differ from a plain program's by a relative error of at most 0.0002.
Values sent between devices are 32-bit elements; how exact they have to be, the bound alone decides.
A program may use at most 64 MiB of HBM per device.

v0:
```python
import functools

import jax
import jax.numpy as jnp
import numpy as np
from jax import lax
from jax.experimental import pallas as pl
from jax.experimental.pallas import tpu as pltpu
from jax.sharding import PartitionSpec as P


def element_matrix():
    ratio = 0.3
    lame = ratio / ((1.0 + ratio) * (1.0 - 2.0 * ratio))
    shear = 1.0 / (2.0 * (1.0 + ratio))
    elastic = np.zeros((6, 6))
    elastic[:3, :3] = lame
    for index in range(3):
        elastic[index, index] = lame + 2.0 * shear
        elastic[index + 3, index + 3] = shear
    points = [0.5 - 0.5 / np.sqrt(3.0), 0.5 + 0.5 / np.sqrt(3.0)]
    result = np.zeros((24, 24))
    for gx in points:
        for gy in points:
            for gz in points:
                strain_map = np.zeros((6, 24))
                for a in range(2):
                    for b in range(2):
                        for c in range(2):
                            node = 4 * a + 2 * b + c
                            fx = gx if a else 1.0 - gx
                            fy = gy if b else 1.0 - gy
                            fz = gz if c else 1.0 - gz
                            sx = 1.0 if a else -1.0
                            sy = 1.0 if b else -1.0
                            sz = 1.0 if c else -1.0
                            dxn = sx * fy * fz
                            dyn = fx * sy * fz
                            dzn = fx * fy * sz
                            strain_map[0, node] = dxn
                            strain_map[1, 8 + node] = dyn
                            strain_map[2, 16 + node] = dzn
                            strain_map[3, 8 + node] = dzn
                            strain_map[3, 16 + node] = dyn
                            strain_map[4, node] = dzn
                            strain_map[4, 16 + node] = dxn
                            strain_map[5, node] = dyn
                            strain_map[5, 8 + node] = dxn
                result = result + strain_map.T @ elastic @ strain_map / 8.0
    return result


def strain_table():
    table = np.zeros((6, 24))
    for a in range(2):
        for b in range(2):
            for c in range(2):
                node = 4 * a + 2 * b + c
                table[0, node] = a
                table[1, 8 + node] = b
                table[2, 16 + node] = c
                table[3, 8 + node] = 0.5 * c
                table[3, 16 + node] = 0.5 * b
                table[4, node] = 0.5 * c
                table[4, 16 + node] = 0.5 * a
                table[5, node] = 0.5 * b
                table[5, 8 + node] = 0.5 * a
    return table


def mode_factor():
    butterfly = np.array([[1.0, 1.0], [-1.0, 1.0]])
    modes = np.kron(np.eye(3), np.kron(butterfly, np.kron(butterfly, butterfly)))
    left = modes @ element_matrix() @ modes.T / 64.0
    rows = []
    for index in range(24):
        if left[index, index] > 1e-9:
            row = left[index] / np.sqrt(left[index, index])
            row[np.abs(row) < 1e-9] = 0.0
            rows.append(row)
            left = left - np.outer(row, row)
    factor = np.stack(rows)
    unit = strain_table() @ modes.T @ factor.T
    unit[np.abs(unit) < 1e-9] = 0.0
    rows = [[(int(i), float(row[i])) for i in np.nonzero(row)[0]] for row in factor]
    columns = [
        [(j, float(factor[j, i])) for j in range(len(rows)) if factor[j, i] != 0.0]
        for i in range(24)
    ]
    return rows, columns, unit


ROWS, COLUMNS, UNIT = mode_factor()
TERMS = len(ROWS)
PAIRS = [(i, j) for i in range(8) for j in range(i, 8)]


def total_of(terms):
    return functools.reduce(lambda x, y: x + y, terms)


def plane_modes(v):
    ahead = pltpu.roll(v, v.shape[1] - 1, 1)
    result = [None] * 4
    for c, part in enumerate((v + ahead, ahead - v)):
        up = pltpu.roll(part, v.shape[0] - 1, 0)
        result[c] = part + up
        result[2 + c] = up - part
    return result


def plane_spread(g):
    sums = [g[c] - g[2 + c] + pltpu.roll(g[c] + g[2 + c], 1, 0) for c in range(2)]
    return sums[0] - sums[1] + pltpu.roll(sums[0] + sums[1], 1, 1)


def cell_terms(lower, upper):
    modes = {}
    for comp in range(3):
        for bc in range(4):
            lo, hi = lower[comp * 4 + bc], upper[comp * 4 + bc]
            modes[comp * 8 + bc] = lo + hi
            modes[comp * 8 + 4 + bc] = hi - lo
    return [total_of([weight * modes[i] for i, weight in row]) for row in ROWS]


def cell_spread(terms):
    lower, upper = [], []
    for comp in range(3):
        for bc in range(4):
            even = COLUMNS[comp * 8 + bc]
            odd = COLUMNS[comp * 8 + 4 + bc]
            slope = total_of([weight * terms[j] for j, weight in odd])
            if even:
                mean = total_of([weight * terms[j] for j, weight in even])
                lower.append(mean - slope)
                upper.append(mean + slope)
            else:
                lower.append(-slope)
                upper.append(slope)
    return lower, upper


def unit_terms(name):
    result = {}
    for j in range(TERMS):
        picks = [
            jnp.where(name == s, float(UNIT[s, j]), 0.0) for s in range(6) if UNIT[s, j] != 0.0
        ]
        if picks:
            result[j] = total_of(picks)
    return result


def fold(x):
    return jnp.sum(x.reshape(-1, 8, x.shape[-1]), axis=0)


def kernel(
    bricks, groups, table, multiplier, target, steps, density, phase, warm,
    fluct, tensor, gradient,
    moduli, slope, below, above, modes, forces, res, image, packed, fields, terms,
    products, sums, spread, reduced, first, second,
    modulus_send, modulus_recv, warm_send, warm_recv, res_send, res_recv,
    red_send, red_recv, field_send, field_recv, first_send, first_recv, second_send, second_recv,
):
    brick = lax.axis_index("brick")
    group = lax.axis_index("case")
    height, width = warm.shape[3], warm.shape[4]
    slab = height // groups
    up = lax.rem(brick + 1, bricks)
    down = lax.rem(brick + bricks - 1, bricks)

    barrier = pltpu.get_barrier_semaphore()
    for step in range(1, bricks):
        pl.semaphore_signal(
            barrier, inc=1, device_id={"brick": lax.rem(brick + step, bricks)},
            device_id_type=pl.DeviceIdType.MESH,
        )
    for step in range(1, groups):
        pl.semaphore_signal(
            barrier, inc=1, device_id={"case": lax.rem(group + step, groups)},
            device_id_type=pl.DeviceIdType.MESH,
        )

    kind = phase[...]
    scale = 0.5 + 0.5 * (kind >= 1).astype(jnp.float32) + 1.0 * (kind >= 2).astype(jnp.float32)
    square = density[...] * density[...]
    moduli[1:3] = 0.05 + square * density[...] * scale
    slope[...] = 3.0 * square * scale

    pl.semaphore_wait(barrier, bricks + groups - 2)
    pending = []

    def send(src, dst, send_sem, recv_sem, **where):
        copy = pltpu.make_async_remote_copy(
            src_ref=src, dst_ref=dst, send_sem=send_sem, recv_sem=recv_sem,
            device_id=where, device_id_type=pl.DeviceIdType.MESH,
        )
        copy.start()
        pending.append(copy)
        return copy

    modulus_copies = [
        send(moduli.at[1], moduli.at[3], modulus_send.at[0], modulus_recv.at[0], brick=down),
        send(moduli.at[2], moduli.at[0], modulus_send.at[1], modulus_recv.at[1], brick=up),
    ]
    warm_copies = [
        [
            send(warm.at[k, :, 0], above.at[k], warm_send.at[k, 0], warm_recv.at[k, 0], brick=down),
            send(warm.at[k, :, 1], below.at[k], warm_send.at[k, 1], warm_recv.at[k, 1], brick=up),
        ]
        for k in range(2)
    ]

    def into_modes(k, node, values):
        for comp in range(3):
            for bc, part in enumerate(plane_modes(values(comp))):
                modes[k, node, comp * 4 + bc] = part

    def apply(k, first_element, count, constant):
        def chunk(index, carry):
            rows = pl.ds(pl.multiple_of(index * 8, 8), 8)
            lower = [modes[k, 0, i, rows] for i in range(12)]
            before = None
            for e in range(count):
                upper = [modes[k, e + 1, i, rows] for i in range(12)]
                found = cell_terms(lower, upper)
                if constant is not None:
                    found = [
                        constant[j] - z if j in constant else -z for j, z in enumerate(found)
                    ]
                modulus = moduli[e, rows]
                on_lower, on_upper = cell_spread([modulus * z for z in found])
                if before is not None:
                    for i in range(12):
                        forces[e - 1, i, rows] = before[i] + on_lower[i]
                before = on_upper
                lower = upper
            return carry

        lax.fori_loop(0, height // 8, chunk, 0)

    def node_force(node, comp):
        return plane_spread([forces[node, comp * 4 + bc] for bc in range(4)])

    for k in range(2):
        for node in range(2):
            into_modes(k, node + 1, lambda comp: warm[k, comp, node])
    res_copies = []
    for k in range(2):
        if k == 0:
            for copy in modulus_copies:
                copy.wait_recv()
        for copy in warm_copies[k]:
            copy.wait_recv()
        into_modes(k, 0, lambda comp: below[k, comp])
        into_modes(k, 3, lambda comp: above[k, comp])
        apply(k, 0, 3, unit_terms(table[group * 2 + k]))
        for node in range(2):
            for comp in range(3):
                res[k, node + 1, comp] = node_force(node, comp)
        res_copies.append([
            send(res.at[k, pl.ds(1, 2)], res.at[k, pl.ds(3, 2)], res_send.at[k, 0], res_recv.at[k, 0], brick=down),
            send(res.at[k, 2], res.at[k, 0], res_send.at[k, 1], res_recv.at[k, 1], brick=up),
        ])
    red_copies = []
    for k in range(2):
        for node in (1, 2):
            into_modes(k, node, lambda comp: res[k, node, comp])
        for copy in res_copies[k]:
            copy.wait_recv()
        for node in (0, 3, 4):
            into_modes(k, node, lambda comp: res[k, node, comp])
        apply(k, 0, 4, None)
        squares = [jnp.zeros((8, width), jnp.float32) for _ in range(3)]
        for node in range(3):
            for comp in range(3):
                value = node_force(node, comp)
                image[k, node, comp] = value
                for bc, part in enumerate(plane_modes(value)):
                    modes[k, node, comp * 4 + bc] = part
                if node < 2:
                    own = res[k, node + 1, comp]
                    squares[0] += fold(own * own)
                    squares[1] += fold(own * value)
                    squares[2] += fold(value * value)

        def energy(index, carry):
            rows = pl.ds(pl.multiple_of(index * 8, 8), 8)
            lower = [modes[k, 0, i, rows] for i in range(12)]
            for e in range(2):
                upper = [modes[k, e + 1, i, rows] for i in range(12)]
                found = cell_terms(lower, upper)
                carry = carry + moduli[e + 1, rows] * total_of([z * z for z in found])
                lower = upper
            return carry

        squares.append(lax.fori_loop(0, height // 8, energy, jnp.zeros((8, width), jnp.float32)))
        lines = [jnp.sum(s, axis=0, keepdims=True) for s in squares]
        lines.append(jnp.zeros((4, width), jnp.float32))
        reduced[k, brick] = jnp.concatenate(lines, axis=0)
        red_copies.append([
            send(
                reduced.at[k, brick], reduced.at[k, brick], red_send.at[k, step - 1],
                red_recv.at[k, step - 1], brick=lax.rem(brick + step, bricks),
            )
            for step in range(1, bricks)
        ])
    field_copies = []
    for k in range(2):
        for copy in red_copies[k]:
            copy.wait_recv()
        moments = jnp.sum(jnp.sum(reduced[k], axis=0), axis=1, keepdims=True)
        rr, rar, pp, pap = (moments[i : i + 1] for i in range(4))
        alpha = rr / rar
        later = alpha * alpha * pp - rr
        grow = 1.0 + later / rr
        curve = grow * grow * rar - 2.0 * grow * alpha * pp + alpha * alpha * pap
        alpha_later = later / curve
        on_res = alpha + alpha_later * grow
        on_image = -alpha_later * alpha
        for node in range(3):
            for comp in range(3):
                start = above[k, comp] if node == 2 else warm[k, comp, node]
                value = start + on_res * res[k, node + 1, comp] + on_image * image[k, node, comp]
                if node < 2:
                    fluct[k, comp, node] = value
                place = node * 3 + comp
                for g in range(groups):
                    packed[k, g, place * slab : (place + 1) * slab] = value[g * slab : (g + 1) * slab]
                    edge = (g + 1) * slab % height
                    packed[k, g, 9 * slab + place : 9 * slab + place + 1] = value[edge : edge + 1]
        for g in range(groups):
            packed[k, g, 9 * slab + 9 : 9 * slab + 16] = jnp.zeros((7, width), jnp.float32)
        field_copies.append([])
        for step in range(1, groups):
            peer = lax.rem(group + step, groups)
            field_copies[k].append(send(
                packed.at[k, peer], fields.at[group * 2 + k], field_send.at[k, step - 1],
                field_recv.at[k, step - 1], case=peer,
            ))
        fields[group * 2 + k] = packed[k, group]

    last = lax.broadcasted_iota(jnp.int32, (slab, width), 0) == slab - 1

    def case_terms(k, which):
        constant = unit_terms(table[which])
        lower = None
        for node in range(3):
            upper = []
            for comp in range(3):
                place = node * 3 + comp
                v = fields[which, place * slab : (place + 1) * slab]
                edge = fields[which, 9 * slab + place : 9 * slab + place + 1]
                next_v = jnp.where(last, edge, pltpu.roll(v, slab - 1, 0))
                ahead, next_ahead = pltpu.roll(v, width - 1, 1), pltpu.roll(next_v, width - 1, 1)
                s, d = v + ahead, ahead - v
                ns, nd = next_v + next_ahead, next_ahead - next_v
                upper += [s + ns, d + nd, ns - s, nd - d]
            if lower is not None:
                found = cell_terms(lower, upper)
                for j, z in enumerate(found):
                    terms[which, j, node - 1] = constant[j] - z if j in constant else -z
            lower = upper

    for k in range(2):
        case_terms(k, group * 2 + k)
    for k in range(2):
        for step in range(1, groups):
            field_copies[k][step - 1].wait_recv()
            case_terms(k, lax.rem(group + groups - step, groups) * 2 + k)

    own_rows = pl.ds(pl.multiple_of(group * slab, slab), slab)
    own_moduli = moduli[1:3, own_rows]
    for index, (i, j) in enumerate(PAIRS):
        value = terms[i, 0] * terms[j, 0]
        for t in range(1, TERMS):
            value = value + terms[i, t] * terms[j, t]
        products[index] = value
        line = jnp.sum(fold((value * own_moduli).reshape(2 * slab, width)), axis=0, keepdims=True)
        sums[i * 8 + j : i * 8 + j + 1] = line
        if i != j:
            sums[j * 8 + i : j * 8 + i + 1] = line
    totals = jnp.sum(sums[...], axis=1, keepdims=True)
    lane = lax.broadcasted_iota(jnp.int32, (8, width), 1)
    row = lax.broadcasted_iota(jnp.int32, (8, width), 0)
    tile = jnp.zeros((8, width), jnp.float32)
    for i in range(8):
        line = jnp.sum(jnp.where(lane == row, totals[i * 8 : i * 8 + 8], 0.0), axis=0, keepdims=True)
        tile = jnp.where(row == i, line, tile)
    first[group] = tile
    copies = [
        send(first.at[group], first.at[group], first_send.at[step - 1], first_recv.at[step - 1], case=lax.rem(group + step, groups))
        for step in range(1, groups)
    ]
    for copy in copies:
        copy.wait_recv()
    second[brick] = jnp.sum(first[...], axis=0)
    copies = [
        send(second.at[brick], second.at[brick], second_send.at[step - 1], second_recv.at[step - 1], brick=lax.rem(brick + step, bricks))
        for step in range(1, bricks)
    ]
    for copy in copies:
        copy.wait_recv()
    tile = jnp.sum(second[...], axis=0) * (1.0 / (bricks * 2 * height * width))
    for k in range(2):
        line = jnp.sum(jnp.where(row == group * 2 + k, tile, 0.0), axis=0, keepdims=True)
        tensor[k : k + 1] = line[:, :8]
    for i in range(8):
        picked = jnp.where(lane == row, jnp.broadcast_to(tile[i : i + 1], (8, width)), 0.0)
        spread[i * 8 : i * 8 + 8] = jnp.broadcast_to(jnp.sum(picked, axis=1, keepdims=True), (8, width))

    def weight(i, j):
        penalty = 0.25 * (jnp.int32(1) << steps[i, j]).astype(jnp.float32)
        return multiplier[i, j] + penalty * (spread[i * 8 + j : i * 8 + j + 1] - target[i, j])

    active = [jnp.where(table[i] < 6, 1.0, 0.0) for i in range(8)]
    result = jnp.zeros((2, slab, width), jnp.float32)
    for index, (i, j) in enumerate(PAIRS):
        both = weight(i, j) if i == j else weight(i, j) + weight(j, i)
        both = (active[i] * active[j]) * both
        result = result + both[None] * products[index]
    gradient[...] = slope[:, own_rows] * result
    for copy in pending:
        copy.wait_send()


def on_device(bricks, groups, density, phase, warm_start, case_table, multiplier, target, penalty_steps):
    height, width = density.shape[1:]
    slab = height // groups
    f32 = jnp.float32
    vmem = pl.BlockSpec(memory_space=pltpu.VMEM)
    smem = pl.BlockSpec(memory_space=pltpu.SMEM)
    dma = pltpu.SemaphoreType.DMA
    return pl.pallas_call(
        functools.partial(kernel, bricks, groups),
        out_shape=(
            jax.ShapeDtypeStruct(warm_start.shape, f32),
            jax.ShapeDtypeStruct((2, 8), f32),
            jax.ShapeDtypeStruct((2, slab, width), f32),
        ),
        in_specs=[smem] * 4 + [vmem] * 3,
        out_specs=(vmem,) * 3,
        scratch_shapes=[
            pltpu.VMEM((4, height, width), f32),
            pltpu.VMEM((2, height, width), f32),
            pltpu.VMEM((2, 3, height, width), f32),
            pltpu.VMEM((2, 3, height, width), f32),
            pltpu.VMEM((2, 5, 12, height, width), f32),
            pltpu.VMEM((3, 12, height, width), f32),
            pltpu.VMEM((2, 5, 3, height, width), f32),
            pltpu.VMEM((2, 3, 3, height, width), f32),
            pltpu.VMEM((2, groups, 9 * slab + 16, width), f32),
            pltpu.VMEM((8, 9 * slab + 16, width), f32),
            pltpu.VMEM((8, TERMS, 2, slab, width), f32),
            pltpu.VMEM((len(PAIRS), 2, slab, width), f32),
            pltpu.VMEM((64, width), f32),
            pltpu.VMEM((64, width), f32),
            pltpu.VMEM((2, bricks, 8, width), f32),
            pltpu.VMEM((groups, 8, width), f32),
            pltpu.VMEM((bricks, 8, width), f32),
            dma((2,)), dma((2,)),
            dma((2, 2)), dma((2, 2)),
            dma((2, 2)), dma((2, 2)),
            dma((2, bricks - 1)), dma((2, bricks - 1)),
            dma((2, groups - 1)), dma((2, groups - 1)),
            dma((groups - 1,)), dma((groups - 1,)),
            dma((bricks - 1,)), dma((bricks - 1,)),
        ],
        compiler_params=pltpu.CompilerParams(
            collective_id=0, has_side_effects=True, vmem_limit_bytes=40 * 2**20
        ),
    )(case_table, multiplier, target, penalty_steps, density, phase, warm_start)


def solution(mesh):
    return jax.shard_map(
        functools.partial(on_device, mesh.shape["brick"], mesh.shape["case"]),
        mesh=mesh,
        in_specs=(
            P(("parts", "brick"), None, None),
            P(("parts", "brick"), None, None),
            P(("parts", "case"), None, "brick", None, None),
            P(),
            P(),
            P(),
            P(),
        ),
        out_specs=(
            P(("parts", "case"), None, "brick", None, None),
            P(("parts", "case"), None),
            P(("parts", "brick"), "case", None),
        ),
        check_vma=False,
    )
```

profile of v0, /device:TPU:0, one launch (start us, length us, event | category | flops | bytes accessed | tf_op | source)
XLA Modules:
  0.0 56.0 jit_solution(12362783374121505792)
XLA Ops:
  0.6 0.0 copy-start
  0.6 1.0 %copy-done = f32[2,3,2,64,128]{4,3,2,1,0:T(8,128)S(1)} copy-done((f32[2,3,2,64,128]{4,3,2,1,0:T(8,128)S(1)}, f32[2,3,2,64,128]{4,3,2,1,0:T(8,128)}, u32[]{:S(2)}) %copy-start) | copy-done | bytes 393240
  1.6 0.0 copy-start.1
  1.6 0.8 %copy-done.1 = f32[2,64,128]{2,1,0:T(8,128)S(1)} copy-done((f32[2,64,128]{2,1,0:T(8,128)S(1)}, f32[2,64,128]{2,1,0:T(8,128)}, u32[]{:S(2)}) %copy-start.1) | copy-done | bytes 65560
  2.5 0.0 copy-start.2
  2.5 0.8 %copy-done.2 = s32[2,64,128]{2,1,0:T(8,128)S(1)} copy-done((s32[2,64,128]{2,1,0:T(8,128)S(1)}, s32[2,64,128]{2,1,0:T(8,128)}, u32[]{:S(2)}) %copy-start.2) | copy-done | bytes 65560
  3.3 0.0 copy-start.3
  3.3 0.7 %copy-done.3 = f32[8,8]{1,0:T(8,128)S(1)} copy-done((f32[8,8]{1,0:T(8,128)S(1)}, f32[8,8]{1,0:T(8,128)}, u32[]{:S(2)}) %copy-start.3) | copy-done | bytes 280
  4.0 0.0 copy-start.4
  4.0 0.7 %copy-done.4 = f32[8,8]{1,0:T(8,128)S(1)} copy-done((f32[8,8]{1,0:T(8,128)S(1)}, f32[8,8]{1,0:T(8,128)}, u32[]{:S(2)}) %copy-start.4) | copy-done | bytes 280
  4.7 0.0 copy-start.5
  4.7 0.7 %copy-done.5 = s32[8,8]{1,0:T(8,128)S(1)} copy-done((s32[8,8]{1,0:T(8,128)S(1)}, s32[8,8]{1,0:T(8,128)}, u32[]{:S(2)}) %copy-start.5) | copy-done | bytes 280
  5.4 0.0 copy-start.6
  5.4 0.7 %copy-done.6 = s32[8]{0:T(128)S(1)} copy-done((s32[8]{0:T(128)S(1)}, s32[8]{0:T(128)}, u32[]{:S(2)}) %copy-start.6) | copy-done | bytes 56
  6.0 48.0 %shard_map.94 = (f32[2,3,2,64,128]{4,3,2,1,0:T(8,128)S(1)}, f32[2,8]{1,0:T(2,128)S(1)}, f32[2,16,128]{2,1,0:T(8,128)S(1)}) custom-call(s32[8]{0:T(128)S(1)} %copy-done.6, f32[8,8]{1,0:T(8,128)S(1)} %copy-done.3, f32[8,8]{1,0:T(8,128)S(1)} %copy-done.4, s32[8,8]{1,0:T(8,128)S(1)} %copy-done.5, f32[2,64,128]{2,1,0:T(8,128)S(1)} %copy-done.1, ...), custom_call_target="tpu_custom_call" | custom-call | tf_op jit(solution)/shard_map/pallas_call | solution.py:436
  54.1 0.7 %copy.13 = f32[2,3,2,64,128]{4,3,2,1,0:T(8,128)} copy(f32[2,3,2,64,128]{4,3,2,1,0:T(8,128)S(1)} %get-tuple-element.6) | data formatting | bytes 786432
  54.8 0.6 %copy.14 = f32[2,8]{1,0:T(2,128)} copy(f32[2,8]{1,0:T(2,128)S(1)} %get-tuple-element.7) | data formatting | bytes 128
  55.4 0.6 %copy.15 = f32[2,16,128]{2,1,0:T(8,128)} copy(f32[2,16,128]{2,1,0:T(8,128)S(1)} %get-tuple-element.8) | data formatting | bytes 32768
Async XLA Ops:
  0.6 1.0 %copy-start = (f32[2,3,2,64,128]{4,3,2,1,0:T(8,128)S(1)}, f32[2,3,2,64,128]{4,3,2,1,0:T(8,128)}, u32[]{:S(2)}) copy-start(f32[2,3,2,64,128]{4,3,2,1,0:T(8,128)} %warm.1) | copy-start | bytes 1179652
  1.6 0.8 %copy-start.1 = (f32[2,64,128]{2,1,0:T(8,128)S(1)}, f32[2,64,128]{2,1,0:T(8,128)}, u32[]{:S(2)}) copy-start(f32[2,64,128]{2,1,0:T(8,128)} %density.1) | copy-start | bytes 196612
  2.5 0.8 %copy-start.2 = (s32[2,64,128]{2,1,0:T(8,128)S(1)}, s32[2,64,128]{2,1,0:T(8,128)}, u32[]{:S(2)}) copy-start(s32[2,64,128]{2,1,0:T(8,128)} %phase.1) | copy-start | bytes 196612
  3.3 0.7 %copy-start.3 = (f32[8,8]{1,0:T(8,128)S(1)}, f32[8,8]{1,0:T(8,128)}, u32[]{:S(2)}) copy-start(f32[8,8]{1,0:T(8,128)} %multiplier.1) | copy-start | bytes 772
  4.0 0.7 %copy-start.4 = (f32[8,8]{1,0:T(8,128)S(1)}, f32[8,8]{1,0:T(8,128)}, u32[]{:S(2)}) copy-start(f32[8,8]{1,0:T(8,128)} %target.1) | copy-start | bytes 772
  4.7 0.7 %copy-start.5 = (s32[8,8]{1,0:T(8,128)S(1)}, s32[8,8]{1,0:T(8,128)}, u32[]{:S(2)}) copy-start(s32[8,8]{1,0:T(8,128)} %steps.1) | copy-start | bytes 772
  5.4 0.7 %copy-start.6 = (s32[8]{0:T(128)S(1)}, s32[8]{0:T(128)}, u32[]{:S(2)}) copy-start(s32[8]{0:T(128)} %table.1) | copy-start | bytes 100
where the time goes:
time: 56.3 us; the launch traced here: 56 us
  Pallas kernels  48 us (85%)
  local copies, waits for them, and re-layouts  7.3 us (13%)
  between operations  0.66 us (1%)
    pallas_call x1, Pallas kernels, on_device(): pl.pallas_call(functools.partial(kernel, bricks, groups), out_shape=(jax....  48 us
    unnamed x17, local copies, waits for them, and re-layouts  7.3 us

commit v1 on v0

--- a/solution.py
+++ b/solution.py
@@ -157,12 +157,13 @@
 
 
 def kernel(
-    bricks, groups, table, multiplier, target, steps, density, phase, warm,
+    bricks, groups, table_in, multiplier_in, target_in, steps_in, density_in, phase_in, warm_in,
     fluct, tensor, gradient,
+    table, multiplier, target, steps, density, phase, warm,
     moduli, slope, below, above, modes, forces, res, image, packed, fields, terms,
-    products, sums, spread, reduced, first, second,
+    products, sums, spread, reduced, second,
     modulus_send, modulus_recv, warm_send, warm_recv, res_send, res_recv,
-    red_send, red_recv, field_send, field_recv, first_send, first_recv, second_send, second_recv,
+    red_send, red_recv, field_send, field_recv, second_send, second_recv, in_sem,
 ):
     brick = lax.axis_index("brick")
     group = lax.axis_index("case")
@@ -171,25 +172,37 @@
     up = lax.rem(brick + 1, bricks)
     down = lax.rem(brick + bricks - 1, bricks)
 
+    peers = [(i, j) for i in range(bricks) for j in range(groups) if (i, j) != (0, 0)]
+
+    def place_of(step):
+        return {
+            "brick": lax.rem(brick + step[0], bricks), "case": lax.rem(group + step[1], groups)
+        }
+
+    loads = [
+        pltpu.make_async_copy(src, dst, in_sem.at[i])
+        for i, (src, dst) in enumerate([
+            (density_in, density), (phase_in, phase), (warm_in, warm), (table_in, table),
+            (multiplier_in, multiplier), (target_in, target), (steps_in, steps),
+        ])
+    ]
+    for load in loads:
+        load.start()
     barrier = pltpu.get_barrier_semaphore()
-    for step in range(1, bricks):
+    for step in peers:
         pl.semaphore_signal(
-            barrier, inc=1, device_id={"brick": lax.rem(brick + step, bricks)},
-            device_id_type=pl.DeviceIdType.MESH,
+            barrier, inc=1, device_id=place_of(step), device_id_type=pl.DeviceIdType.MESH
         )
-    for step in range(1, groups):
-        pl.semaphore_signal(
-            barrier, inc=1, device_id={"case": lax.rem(group + step, groups)},
-            device_id_type=pl.DeviceIdType.MESH,
-        )
-
+
+    for load in loads:
+        load.wait()
     kind = phase[...]
     scale = 0.5 + 0.5 * (kind >= 1).astype(jnp.float32) + 1.0 * (kind >= 2).astype(jnp.float32)
     square = density[...] * density[...]
     moduli[1:3] = 0.05 + square * density[...] * scale
     slope[...] = 3.0 * square * scale
 
-    pl.semaphore_wait(barrier, bricks + groups - 2)
+    pl.semaphore_wait(barrier, len(peers))
     pending = []
 
     def send(src, dst, send_sem, recv_sem, **where):
@@ -264,8 +277,9 @@
             send(res.at[k, pl.ds(1, 2)], res.at[k, pl.ds(3, 2)], res_send.at[k, 0], res_recv.at[k, 0], brick=down),
             send(res.at[k, 2], res.at[k, 0], res_send.at[k, 1], res_recv.at[k, 1], brick=up),
         ])
-    red_copies = []
-    for k in range(2):
+    red_copies, field_copies = [], []
+
+    def second_image(k):
         for node in (1, 2):
             into_modes(k, node, lambda comp: res[k, node, comp])
         for copy in res_copies[k]:
@@ -307,8 +321,7 @@
             )
             for step in range(1, bricks)
         ])
-    field_copies = []
-    for k in range(2):
+    def finish(k):
         for copy in red_copies[k]:
             copy.wait_recv()
         moments = jnp.sum(jnp.sum(reduced[k], axis=0), axis=1, keepdims=True)
@@ -364,24 +377,37 @@
                     terms[which, j, node - 1] = constant[j] - z if j in constant else -z
             lower = upper
 
-    for k in range(2):
-        case_terms(k, group * 2 + k)
-    for k in range(2):
+    own_rows = pl.ds(pl.multiple_of(group * slab, slab), slab)
+    own_moduli = moduli[1:3, own_rows]
+
+    def pair_products(chosen):
+        for i, j in chosen:
+            value = terms[i, 0] * terms[j, 0]
+            for t in range(1, TERMS):
+                value = value + terms[i, t] * terms[j, t]
+            products[PAIRS.index((i, j))] = value
+            line = fold((value * own_moduli).reshape(2 * slab, width))
+            line = jnp.sum(line, axis=0, keepdims=True)
+            sums[i * 8 + j : i * 8 + j + 1] = line
+            if i != j:
+                sums[j * 8 + i : j * 8 + i + 1] = line
+
+    def arrived_terms(k):
         for step in range(1, groups):
             field_copies[k][step - 1].wait_recv()
             case_terms(k, lax.rem(group + groups - step, groups) * 2 + k)
 
-    own_rows = pl.ds(pl.multiple_of(group * slab, slab), slab)
-    own_moduli = moduli[1:3, own_rows]
-    for index, (i, j) in enumerate(PAIRS):
-        value = terms[i, 0] * terms[j, 0]
-        for t in range(1, TERMS):
-            value = value + terms[i, t] * terms[j, t]
-        products[index] = value
-        line = jnp.sum(fold((value * own_moduli).reshape(2 * slab, width)), axis=0, keepdims=True)
-        sums[i * 8 + j : i * 8 + j + 1] = line
-        if i != j:
-            sums[j * 8 + i : j * 8 + i + 1] = line
+    early = [pair for pair in PAIRS if pair[0] % 2 == 0 and pair[1] % 2 == 0]
+    second_image(0)
+    finish(0)
+    case_terms(0, group * 2)
+    second_image(1)
+    arrived_terms(0)
+    finish(1)
+    pair_products(early)
+    case_terms(1, group * 2 + 1)
+    arrived_terms(1)
+    pair_products([pair for pair in PAIRS if pair not in early])
     totals = jnp.sum(sums[...], axis=1, keepdims=True)
     lane = lax.broadcasted_iota(jnp.int32, (8, width), 1)
     row = lax.broadcasted_iota(jnp.int32, (8, width), 0)
@@ -389,17 +415,11 @@
     for i in range(8):
         line = jnp.sum(jnp.where(lane == row, totals[i * 8 : i * 8 + 8], 0.0), axis=0, keepdims=True)
         tile = jnp.where(row == i, line, tile)
-    first[group] = tile
+    mine = brick * groups + group
+    second[mine] = tile
     copies = [
-        send(first.at[group], first.at[group], first_send.at[step - 1], first_recv.at[step - 1], case=lax.rem(group + step, groups))
-        for step in range(1, groups)
-    ]
-    for copy in copies:
-        copy.wait_recv()
-    second[brick] = jnp.sum(first[...], axis=0)
-    copies = [
-        send(second.at[brick], second.at[brick], second_send.at[step - 1], second_recv.at[step - 1], brick=lax.rem(brick + step, bricks))
-        for step in range(1, bricks)
+        send(second.at[mine], second.at[mine], second_send.at[i], second_recv.at[i], **place_of(step))
+        for i, step in enumerate(peers)
     ]
     for copy in copies:
         copy.wait_recv()
@@ -431,7 +451,7 @@
     slab = height // groups
     f32 = jnp.float32
     vmem = pl.BlockSpec(memory_space=pltpu.VMEM)
-    smem = pl.BlockSpec(memory_space=pltpu.SMEM)
+    hbm = pl.BlockSpec(memory_space=pltpu.HBM)
     dma = pltpu.SemaphoreType.DMA
     return pl.pallas_call(
         functools.partial(kernel, bricks, groups),
@@ -440,9 +460,16 @@
             jax.ShapeDtypeStruct((2, 8), f32),
             jax.ShapeDtypeStruct((2, slab, width), f32),
         ),
-        in_specs=[smem] * 4 + [vmem] * 3,
+        in_specs=[hbm] * 7,
         out_specs=(vmem,) * 3,
         scratch_shapes=[
+            pltpu.SMEM((8,), jnp.int32),
+            pltpu.SMEM((8, 8), f32),
+            pltpu.SMEM((8, 8), f32),
+            pltpu.SMEM((8, 8), jnp.int32),
+            pltpu.VMEM(density.shape, f32),
+            pltpu.VMEM(phase.shape, jnp.int32),
+            pltpu.VMEM(warm_start.shape, f32),
             pltpu.VMEM((4, height, width), f32),
             pltpu.VMEM((2, height, width), f32),
             pltpu.VMEM((2, 3, height, width), f32),
@@ -458,15 +485,14 @@
             pltpu.VMEM((64, width), f32),
             pltpu.VMEM((64, width), f32),
             pltpu.VMEM((2, bricks, 8, width), f32),
-            pltpu.VMEM((groups, 8, width), f32),
-            pltpu.VMEM((bricks, 8, width), f32),
+            pltpu.VMEM((bricks * groups, 8, width), f32),
             dma((2,)), dma((2,)),
             dma((2, 2)), dma((2, 2)),
             dma((2, 2)), dma((2, 2)),
             dma((2, bricks - 1)), dma((2, bricks - 1)),
             dma((2, groups - 1)), dma((2, groups - 1)),
-            dma((groups - 1,)), dma((groups - 1,)),
-            dma((bricks - 1,)), dma((bricks - 1,)),
+            dma((bricks * groups - 1,)), dma((bricks * groups - 1,)),
+            dma((7,)),
         ],
         compiler_params=pltpu.CompilerParams(
             collective_id=0, has_side_effects=True, vmem_limit_bytes=40 * 2**20

time: 56.3 us -> 55.6 us (0.988)
  Pallas kernels: 48 us -> 47.3 us
    pallas_call x1, Pallas kernels: 48 us -> 47.3 us  [on_device(): pl.pallas_call(functools.partial(kernel, bricks, groups), out_shape=(jax....]
where the time goes in v1:
time: 55.6 us; the launch traced here: 55.3 us
  Pallas kernels  47.3 us (85%)
  local copies, waits for them, and re-layouts  7.3 us (13%)
  between operations  0.66 us (1%)
    pallas_call x1, Pallas kernels, on_device(): pl.pallas_call(functools.partial(kernel, bricks, groups), out_shape=(jax....  47.3 us
    unnamed x17, local copies, waits for them, and re-layouts  7.3 us

profile of v1, /device:TPU:0, one launch (start us, length us, event | category | flops | bytes accessed | tf_op | source)
XLA Modules:
  0.0 55.3 jit_solution(15939269305831624144)
XLA Ops:
  0.6 0.0 copy-start
  0.6 1.0 %copy-done = f32[2,3,2,64,128]{4,3,2,1,0:T(8,128)S(1)} copy-done((f32[2,3,2,64,128]{4,3,2,1,0:T(8,128)S(1)}, f32[2,3,2,64,128]{4,3,2,1,0:T(8,128)}, u32[]{:S(2)}) %copy-start) | copy-done | bytes 393240
  1.6 0.0 copy-start.1
  1.6 0.8 %copy-done.1 = f32[2,64,128]{2,1,0:T(8,128)S(1)} copy-done((f32[2,64,128]{2,1,0:T(8,128)S(1)}, f32[2,64,128]{2,1,0:T(8,128)}, u32[]{:S(2)}) %copy-start.1) | copy-done | bytes 65560
  2.5 0.0 copy-start.2
  2.5 0.8 %copy-done.2 = s32[2,64,128]{2,1,0:T(8,128)S(1)} copy-done((s32[2,64,128]{2,1,0:T(8,128)S(1)}, s32[2,64,128]{2,1,0:T(8,128)}, u32[]{:S(2)}) %copy-start.2) | copy-done | bytes 65560
  3.3 0.0 copy-start.3
  3.3 0.7 %copy-done.3 = f32[8,8]{1,0:T(8,128)S(1)} copy-done((f32[8,8]{1,0:T(8,128)S(1)}, f32[8,8]{1,0:T(8,128)}, u32[]{:S(2)}) %copy-start.3) | copy-done | bytes 280
  4.0 0.0 copy-start.4
  4.0 0.7 %copy-done.4 = f32[8,8]{1,0:T(8,128)S(1)} copy-done((f32[8,8]{1,0:T(8,128)S(1)}, f32[8,8]{1,0:T(8,128)}, u32[]{:S(2)}) %copy-start.4) | copy-done | bytes 280
  4.7 0.0 copy-start.5
  4.7 0.7 %copy-done.5 = s32[8,8]{1,0:T(8,128)S(1)} copy-done((s32[8,8]{1,0:T(8,128)S(1)}, s32[8,8]{1,0:T(8,128)}, u32[]{:S(2)}) %copy-start.5) | copy-done | bytes 280
  5.4 0.0 copy-start.6
  5.4 0.7 %copy-done.6 = s32[8]{0:T(128)S(1)} copy-done((s32[8]{0:T(128)S(1)}, s32[8]{0:T(128)}, u32[]{:S(2)}) %copy-start.6) | copy-done | bytes 56
  6.0 47.3 %shard_map.94 = (f32[2,3,2,64,128]{4,3,2,1,0:T(8,128)S(1)}, f32[2,8]{1,0:T(2,128)S(1)}, f32[2,16,128]{2,1,0:T(8,128)S(1)}) custom-call(s32[8]{0:T(128)S(1)} %copy-done.6, f32[8,8]{1,0:T(8,128)S(1)} %copy-done.3, f32[8,8]{1,0:T(8,128)S(1)} %copy-done.4, s32[8,8]{1,0:T(8,128)S(1)} %copy-done.5, f32[2,64,128]{2,1,0:T(8,128)S(1)} %copy-done.1, ...), custom_call_target="tpu_custom_call" | custom-call | tf_op jit(solution)/shard_map/pallas_call | solution.py:456
  53.4 0.7 %copy.13 = f32[2,3,2,64,128]{4,3,2,1,0:T(8,128)} copy(f32[2,3,2,64,128]{4,3,2,1,0:T(8,128)S(1)} %get-tuple-element.6) | data formatting | bytes 786432
  54.1 0.6 %copy.14 = f32[2,8]{1,0:T(2,128)} copy(f32[2,8]{1,0:T(2,128)S(1)} %get-tuple-element.7) | data formatting | bytes 128
  54.7 0.6 %copy.15 = f32[2,16,128]{2,1,0:T(8,128)} copy(f32[2,16,128]{2,1,0:T(8,128)S(1)} %get-tuple-element.8) | data formatting | bytes 32768
Async XLA Ops:
  0.6 1.0 %copy-start = (f32[2,3,2,64,128]{4,3,2,1,0:T(8,128)S(1)}, f32[2,3,2,64,128]{4,3,2,1,0:T(8,128)}, u32[]{:S(2)}) copy-start(f32[2,3,2,64,128]{4,3,2,1,0:T(8,128)} %warm_in.1) | copy-start | bytes 1179652
  1.6 0.8 %copy-start.1 = (f32[2,64,128]{2,1,0:T(8,128)S(1)}, f32[2,64,128]{2,1,0:T(8,128)}, u32[]{:S(2)}) copy-start(f32[2,64,128]{2,1,0:T(8,128)} %density_in.1) | copy-start | bytes 196612
  2.5 0.8 %copy-start.2 = (s32[2,64,128]{2,1,0:T(8,128)S(1)}, s32[2,64,128]{2,1,0:T(8,128)}, u32[]{:S(2)}) copy-start(s32[2,64,128]{2,1,0:T(8,128)} %phase_in.1) | copy-start | bytes 196612
  3.3 0.7 %copy-start.3 = (f32[8,8]{1,0:T(8,128)S(1)}, f32[8,8]{1,0:T(8,128)}, u32[]{:S(2)}) copy-start(f32[8,8]{1,0:T(8,128)} %multiplier_in.1) | copy-start | bytes 772
  4.0 0.7 %copy-start.4 = (f32[8,8]{1,0:T(8,128)S(1)}, f32[8,8]{1,0:T(8,128)}, u32[]{:S(2)}) copy-start(f32[8,8]{1,0:T(8,128)} %target_in.1) | copy-start | bytes 772
  4.7 0.7 %copy-start.5 = (s32[8,8]{1,0:T(8,128)S(1)}, s32[8,8]{1,0:T(8,128)}, u32[]{:S(2)}) copy-start(s32[8,8]{1,0:T(8,128)} %steps_in.1) | copy-start | bytes 772
  5.4 0.7 %copy-start.6 = (s32[8]{0:T(128)S(1)}, s32[8]{0:T(128)}, u32[]{:S(2)}) copy-start(s32[8]{0:T(128)} %table_in.1) | copy-start | bytes 100

commit v2 on v1

--- a/solution.py
+++ b/solution.py
@@ -495,7 +495,7 @@
             dma((7,)),
         ],
         compiler_params=pltpu.CompilerParams(
-            collective_id=0, has_side_effects=True, vmem_limit_bytes=40 * 2**20
+            collective_id=0, has_side_effects=True, vmem_limit_bytes=63 * 2**20 + 2**19
         ),
     )(case_table, multiplier, target, penalty_steps, density, phase, warm_start)
 

time: 55.6 us -> 51.6 us (0.928)
  local copies, waits for them, and re-layouts: 7.3 us -> 2.95 us
    unnamed x17 -> x7, local copies, waits for them, and re-layouts: 7.3 us -> 2.95 us
where the time goes in v2:
time: 51.6 us; the launch traced here: 51.4 us
  Pallas kernels  47.8 us (93%)
  local copies, waits for them, and re-layouts  2.95 us (6%)
  between operations  0.66 us (1%)
    pallas_call x1, Pallas kernels, on_device(): pl.pallas_call(functools.partial(kernel, bricks, groups), out_shape=(jax....  47.8 us
    unnamed x7, local copies, waits for them, and re-layouts  2.95 us

profile of v2, /device:TPU:0, one launch (start us, length us, event | category | flops | bytes accessed | tf_op | source)
XLA Modules:
  0.0 51.4 jit_solution(16796617614702048760)
XLA Ops:
  0.6 47.8 %shard_map.94 = (f32[2,3,2,64,128]{4,3,2,1,0:T(8,128)}, f32[2,8]{1,0:T(2,128)}, f32[2,16,128]{2,1,0:T(8,128)}) custom-call(s32[8]{0:T(128)} %table_in.1, f32[8,8]{1,0:T(8,128)} %multiplier_in.1, f32[8,8]{1,0:T(8,128)} %target_in.1, s32[8,8]{1,0:T(8,128)} %steps_in.1, f32[2,64,128]{2,1,0:T(8,128)} %density_in.1, s32[2,64,128]{2,1,0:T(8,128)} %phase_in.1, ...), custom_call_target="tpu_custom_call" | custom-call | tf_op jit(solution)/shard_map/pallas_call | solution.py:456
  48.4 0.0 copy-start.1
  48.5 0.0 copy-start
  48.5 1.8 %copy.13 = f32[2,3,2,64,128]{4,3,2,1,0:T(8,128)} copy(f32[2,3,2,64,128]{4,3,2,1,0:T(8,128)} %get-tuple-element.6) | data formatting | bytes 786432
  50.2 0.0 copy-done.1
  50.2 0.6 %copy.14 = f32[2,8]{1,0:T(2,128)} copy(f32[2,8]{1,0:T(2,128)S(1)} %copy-done.1) | data formatting | bytes 128
  50.8 0.0 copy-done
  50.8 0.6 %copy.15 = f32[2,16,128]{2,1,0:T(8,128)} copy(f32[2,16,128]{2,1,0:T(8,128)S(1)} %copy-done) | data formatting | bytes 32768
Async XLA Ops:
  48.4 1.8 %copy-start.1 = (f32[2,8]{1,0:T(2,128)S(1)}, f32[2,8]{1,0:T(2,128)}, u32[]{:S(2)}) copy-start(f32[2,8]{1,0:T(2,128)} %get-tuple-element.7) | copy-start | bytes 196
  48.5 2.4 %copy-start = (f32[2,16,128]{2,1,0:T(8,128)S(1)}, f32[2,16,128]{2,1,0:T(8,128)}, u32[]{:S(2)}) copy-start(f32[2,16,128]{2,1,0:T(8,128)} %get-tuple-element.8) | copy-start | bytes 49156
